TPU v7x, 32 devices: a whole 2x2x4 slice. The times are simulated.
32 devices in a mesh: ctx: 2 (over y), exp: 4 (over z), tp: 4 (over x, core).
Axes of the slice: x: 2, y: 2, z: 4, core: 2. Of those that a mesh axis runs over, the one named last changes fastest.
Arguments:
- queries: bfloat16 [256, 2048], P('ctx', ('exp', 'tp')), may hold values from -30 to 30
- rotated_key_rows: bfloat16 [256, 512], P('ctx', 'exp'), may hold values from -9 to 9
- value_vector_rows: bfloat16 [256, 512], P('ctx', 'exp'), may hold values from -6 to 6
- residual: bfloat16 [256, 4096], P(('ctx', 'exp', 'tp')), may hold values from -6 to 6
- norm_gain: float32 [4096], replicated, may hold values from 0.25 to 1.75
- out_proj: bfloat16 [2048, 4096], P(('exp', 'tp')), may hold values from -0.125 to 0.125
- expert_ids: int32 [256, 2], P('ctx'), may hold values from 0 to 3, all different within a row; in each aligned block of 128 rows (0 to 127, 128 to 255, ...) at most 128 rows name the same one
- gate_weights: float32 [256, 2], P('ctx'), may hold values from 0.2 to 1
- w_gate: bfloat16 [4, 4096, 14336], P('exp', None, ('ctx', 'tp')), may hold values from -0.09375 to 0.09375
- w_up: bfloat16 [4, 4096, 14336], P('exp', None, ('ctx', 'tp')), may hold values from -0.09375 to 0.09375
- w_down: bfloat16 [4, 14336, 4096], P('exp', ('ctx', 'tp')), may hold values from -0.046875 to 0.046875
Outputs:
- mixed: bfloat16 [256, 4096], P(('ctx', 'exp', 'tp'))
Inputs may be any that keep to these rules, and one draw needn't show every extreme that they name: `expert_ids`: each row names 2 different experts. In each aligned block of 128 rows no expert is named by more than 128 rows, and in some block one expert is named by exactly 128 rows.
All inputs are finite; a program needn't handle non-finite values.
Results may differ from a plain program's by a relative error of at most 0.019.
Values may be sent and summed in bfloat16 or wider, within the bound.
A program may use at most 128 MiB of HBM per device.

v0:
```python
import jax
import jax.numpy as jnp
from jax import lax
from jax.sharding import PartitionSpec as P

HEAD_WIDTH = 128


def normalize(hidden_sum, norm_gain):
    mean_square = jnp.mean(hidden_sum * hidden_sum, axis=-1, keepdims=True)
    return (hidden_sum * lax.rsqrt(mean_square + 1e-05) * norm_gain).astype(jnp.bfloat16)


def local(
    queries,
    rotated_key_rows,
    value_vector_rows,
    residual,
    norm_gain,
    out_proj,
    expert_ids,
    gate_weights,
    w_gate,
    w_up,
    w_down,
):
    block_rows = queries.shape[0]
    query_heads = queries.shape[1] // HEAD_WIDTH
    own_rows = residual.shape[0]
    query_first = lax.axis_index("ctx") * block_rows
    query_pos = query_first + jnp.arange(block_rows, dtype=jnp.int32)
    query_view = queries.reshape(block_rows, query_heads, HEAD_WIDTH)
    score_scale = HEAD_WIDTH ** (-0.5)
    row_top = jnp.full((query_heads, block_rows), -1e30, jnp.float32)
    key_piece = lax.all_gather(rotated_key_rows, "ctx", axis=0, tiled=True)
    value_piece = lax.all_gather(value_vector_rows, "ctx", axis=0, tiled=True)
    scores = (
        jnp.einsum("qhd,kd->hqk", query_view, key_piece, preferred_element_type=jnp.float32)
        * score_scale
    )
    key_pos = jnp.arange(key_piece.shape[0], dtype=jnp.int32)
    visible = (key_pos[None, :] <= query_pos[:, None])[None]
    scores = jnp.where(visible, scores, -1e30)
    new_top = jnp.maximum(row_top, jnp.max(scores, axis=2))
    weights = jnp.where(visible, jnp.exp(scores - new_top[..., None]), 0.0)
    row_sum = jnp.sum(weights, axis=2)
    weighted = jnp.einsum(
        "hqk,kd->hqd", weights.astype(jnp.bfloat16), value_piece, preferred_element_type=jnp.float32
    )
    row_top, row_sum, weighted = (new_top, row_sum, weighted)
    attended = (weighted / row_sum[..., None]).astype(jnp.bfloat16)
    attended = jnp.transpose(attended, (1, 0, 2)).reshape(block_rows, query_heads * HEAD_WIDTH)
    share_index = lax.axis_index("exp") * lax.axis_size("tp") + lax.axis_index("tp")
    row_first = share_index * own_rows
    partial_value = jnp.dot(attended, out_proj, preferred_element_type=jnp.float32)
    own_part = lax.dynamic_slice_in_dim(partial_value, row_first, own_rows, 0) + residual.astype(
        jnp.float32
    )
    placed = lax.dynamic_update_slice_in_dim(partial_value, own_part, row_first, 0)
    summed = lax.psum(placed.astype(jnp.bfloat16), ("exp", "tp")).astype(jnp.float32)
    normed_block = normalize(summed, norm_gain)
    own_sum = lax.dynamic_slice_in_dim(summed, row_first, own_rows, 0)
    my_expert = lax.axis_index("exp")
    matches = expert_ids == my_expert
    chosen = jnp.any(matches, axis=1)
    slot_rank = jnp.cumsum(chosen.astype(jnp.int32)) - 1
    gate_share = jnp.sum(jnp.where(matches, gate_weights, 0.0), axis=1)
    capacity = 2 * expert_ids.shape[1] * block_rows // lax.axis_size("exp")
    slot_ids = jnp.arange(capacity, dtype=jnp.int32)
    selector = ((slot_rank[None, :] == slot_ids[:, None]) & chosen[None, :]).astype(jnp.bfloat16)
    picked = jnp.dot(selector, normed_block, preferred_element_type=jnp.float32).astype(
        jnp.bfloat16
    )
    expert_input = lax.all_gather(picked, "ctx", axis=0, tiled=True)
    gate_matrix = w_gate[0]
    up_matrix = w_up[0]
    down_matrix = w_down[0]
    share_rows = capacity // lax.axis_size("tp")
    gate_out = jnp.dot(expert_input, gate_matrix, preferred_element_type=jnp.float32)
    up_out = jnp.dot(expert_input, up_matrix, preferred_element_type=jnp.float32)
    hidden = (jax.nn.silu(gate_out) * up_out).astype(jnp.bfloat16)
    expert_out = lax.psum_scatter(
        jnp.dot(hidden, down_matrix, preferred_element_type=jnp.float32).astype(jnp.bfloat16),
        ("ctx", "tp"),
        scatter_dimension=0,
        tiled=True,
    )
    slot_here = lax.axis_index("tp") * share_rows + jnp.arange(share_rows, dtype=jnp.int32)
    expanded_heads = jnp.where(
        (slot_rank[:, None] == slot_here[None, :]) & chosen[:, None], gate_share[:, None], 0.0
    )
    expert_wide = expert_out.astype(jnp.float32)
    combined = lax.psum_scatter(
        jnp.dot(expanded_heads, expert_wide, precision=lax.Precision.HIGHEST).astype(jnp.bfloat16),
        ("exp", "tp"),
        scatter_dimension=0,
        tiled=True,
    ).astype(jnp.float32)
    return (own_sum + combined).astype(jnp.bfloat16)


def solution(mesh):
    return jax.shard_map(
        local,
        mesh=mesh,
        in_specs=(
            P("ctx", ("exp", "tp")),
            P("ctx", "exp"),
            P("ctx", "exp"),
            P(("ctx", "exp", "tp"), None),
            P(),
            P(("exp", "tp"), None),
            P("ctx", None),
            P("ctx", None),
            P("exp", None, ("ctx", "tp")),
            P("exp", None, ("ctx", "tp")),
            P("exp", ("ctx", "tp"), None),
        ),
        out_specs=P(("ctx", "exp", "tp"), None),
        check_vma=False,
    )
```

profile of v0, /device:TPU:0, one launch (start us, length us, event | category | flops | bytes accessed | tf_op | source)
XLA Modules:
  0.0 286.0 jit_solution(10823428701457201607)
XLA Ops:
  6.5 5.9 %all_gather.9 = bf16[256,128]{1,0:T(8,128)(2,1)S(1)} all-gather(bf16[128,128]{1,0:T(8,128)(2,1)} %param.12), channel_id=1, replica_groups=mesh['ctx'=2,'exp'=4,'tp'=4] {'ctx'}, dimensions={0}, use_global_device_ids=true | all-gather | bytes 98304 | tf_op jit(solution)/shard_map/all_gather | solution.py:35
  12.5 1.0 fusion.50
  13.4 4.8 %all_gather.10 = bf16[256,128]{1,0:T(8,128)(2,1)S(1)} all-gather(bf16[128,128]{1,0:T(8,128)(2,1)} %param.13), channel_id=1, replica_groups=mesh['ctx'=2,'exp'=4,'tp'=4] {'ctx'}, dimensions={0}, use_global_device_ids=true | all-gather | bytes 98304 | tf_op jit(solution)/shard_map/all_gather | solution.py:36
  18.2 0.1 fusion.22
  18.3 0.6 fusion.18
  18.9 0.0 copy-start.4
  18.9 0.0 copy-start.3
  19.0 1.1 convert_element_type.55
  20.1 0.0 all-reduce.2.cloned.1.call-update
  20.1 0.0 all-gather.2.cloned.1.call-start
  20.2 0.1 copy.13
  20.3 0.2 reduce-window.7
  20.5 0.1 add_reduce_fusion
  20.6 94.5 %all-reduce.2.cloned.1.call-done = bf16[128,4096]{1,0:T(8,128)(2,1)} async-done(((bf16[128,4096]{1,0:T(8,128)(2,1)}), bf16[128,4096]{1,0:T(8,128)(2,1)}) %all-reduce.2.cloned.1.call-update) | async-done | bytes 1048592 | tf_op jit(solution)/shard_map/psum | solution.py:60
  115.1 1.5 multiply_reduce_fusion
  116.6 2.7 convolution_convert_fusion.1
  119.3 0.0 all-gather.2.cloned.1.call-update
  119.3 0.0 reduce-scatter.3.cloned.1.call-start
  119.4 32.5 %all-gather.2.cloned.1.call-done = bf16[256,4096]{1,0:T(8,128)(2,1)} async-done(((bf16[128,4096]{1,0:T(8,128)(2,1)}), bf16[256,4096]{1,0:T(8,128)(2,1)}) %all-gather.2.cloned.1.call-update) | async-done | bytes 2097168 | tf_op jit(solution)/shard_map/all_gather | solution.py:74
  151.9 8.5 %fusion.4 = f32[256,1792]{1,0:T(8,128)S(1)} fusion(bf16[256,4096]{1,0:T(8,128)(2,1)} %all-gather.2.cloned.1.call-done, bf16[1,4096,1792]{2,1,0:T(8,128)(2,1)} %param.19), kind=kOutput, calls=%fused_computation.4 | convolution fusion | flops 3758096384 | bytes 18612224 | tf_op jit(solution)/shard_map/dot_general | solution.py:79
  160.4 0.0 slice-start.2
  160.5 9.4 %fusion.12 = bf16[256,1792]{1,0:T(8,128)(2,1)S(1)} fusion(bf16[256,4096]{1,0:T(8,128)(2,1)S(1)} %copy-done.6, bf16[1,4096,1792]{2,1,0:T(8,128)(2,1)} %param.20, f32[256,1792]{1,0:T(8,128)S(1)} %fusion.4), kind=kOutput, calls=%fused_computation.10 | convolution fusion | flops 3760848896 | bytes 19529728 | tf_op jit(solution)/shard_map/dot_general | solution.py:80
  169.9 5.3 %fusion.6 = bf16[256,4096]{1,0:T(8,128)(2,1)} fusion(bf16[256,1792]{1,0:T(8,128)(2,1)S(1)} %fusion.12, bf16[1,1792,4096]{2,1,0:T(8,128)(2,1)S(1)} %bitcast.36), kind=kOutput, calls=%fused_computation.6 | convolution fusion | flops 3759144960 | bytes 17694720 | tf_op jit(solution)/shard_map/dot_general | solution.py:83
  175.2 0.0 reduce-scatter.3.cloned.1.call-update
  175.2 0.0 reduce-scatter.5.cloned.1.call-start
  175.3 0.6 copy-done.5
  175.9 40.7 %reduce-scatter.3.cloned.1.call-done = bf16[32,4096]{1,0:T(8,128)(2,1)} async-done(((bf16[256,4096]{1,0:T(8,128)(2,1)}), bf16[32,4096]{1,0:T(8,128)(2,1)}) %reduce-scatter.3.cloned.1.call-update) | async-done | bytes 262160 | tf_op jit(solution)/shard_map/reduce_scatter | solution.py:82
  216.6 3.0 %convolution_convert_fusion = bf16[128,4096]{1,0:T(8,128)(2,1)} fusion(bf16[32,4096]{1,0:T(8,128)(2,1)} %reduce-scatter.3.cloned.1.call-done, f32[128]{0:T(128)S(1)} %select_reduce_fusion, s32[32]{0:T(128)S(1)} %iota_add_fusion, s32[128]{0:T(128)S(1)} %add_reduce_fusion, pred[128]{0:T(512)(128)(4,1)S(1)} %fusion.49), kind=kOutput, calls=%fused_computation.7 | convolution fusion | flops 201863168 | bytes 1312000 | tf_op jit(solution)/shard_map/dot_general | solution.py:94
  219.6 0.0 reduce-scatter.5.cloned.1.call-update
  219.6 1.6 convert_element_type.56
  221.2 56.8 %reduce-scatter.5.cloned.1.call-done = bf16[8,4096]{1,0:T(8,128)(2,1)} async-done(((bf16[128,4096]{1,0:T(8,128)(2,1)}), bf16[8,4096]{1,0:T(8,128)(2,1)}) %reduce-scatter.5.cloned.1.call-update) | async-done | bytes 65552 | tf_op jit(solution)/shard_map/reduce_scatter | solution.py:93
  277.9 1.6 add_convert_fusion
  (28 shorter events, 0.1 us)
Async XLA Ops:
  6.5 11.8 %copy-start = (bf16[128,4096]{1,0:T(8,128)(2,1)S(1)}, bf16[128,4096]{1,0:T(8,128)(2,1)}, u32[]{:S(2)}) copy-start(bf16[128,4096]{1,0:T(8,128)(2,1)} %param.16) | copy-start | bytes 3145732
  6.5 12.4 %copy-start.2 = (bf16[8,4096]{1,0:T(8,128)(2,1)S(1)}, bf16[8,4096]{1,0:T(8,128)(2,1)}, u32[]{:S(2)}) copy-start(bf16[8,4096]{1,0:T(8,128)(2,1)} %param.14) | copy-start | bytes 196612
  6.5 108.5 %all-reduce.2.cloned.1.call-start = ((), (), s32[]{:S(2)}) async-start(), calls=%async_computation.2 | async-start | bytes 2097152 | tf_op jit(solution)/shard_map/psum | solution.py:60
  18.9 1.2 copy-start.4
  18.9 97.6 %copy-start.3 = (f32[4096]{0:T(1024)S(1)}, f32[4096]{0:T(1024)}, u32[]{:S(2)}) copy-start(f32[4096]{0:T(1024)} %param.15) | copy-start | bytes 49156
  20.1 131.8 %all-gather.2.cloned.1.call-start = ((), (), s32[]{:S(2)}) async-start(), calls=%async_computation.3 | async-start | bytes 3145728 | tf_op jit(solution)/shard_map/all_gather | solution.py:74
  119.3 97.3 %reduce-scatter.3.cloned.1.call-start = ((), (), s32[]{:S(2)}) async-start(), calls=%async_computation.4 | async-start | bytes 2359296 | tf_op jit(solution)/shard_map/reduce_scatter | solution.py:82
  151.9 8.6 %copy-start.6 = (bf16[256,4096]{1,0:T(8,128)(2,1)S(1)}, bf16[256,4096]{1,0:T(8,128)(2,1)}, u32[]{:S(2)}) copy-start(bf16[256,4096]{1,0:T(8,128)(2,1)} %all-gather.2.cloned.1.call-done) | copy-start | bytes 6291460
  151.9 18.0 %slice-start = ((s8[14680064]{0:T(1024)(128)(4,1)}), s8[4194304]{0:T(1024)(128)(4,1)S(1)}, s32[]{:S(2)}) async-start(s8[14680064]{0:T(1024)(128)(4,1)} %bitcast.35), calls=%async_computation.6 | async-start | bytes 8388608
  151.9 18.0 %slice-start.1 = ((s8[14680064]{0:T(1024)(128)(4,1)}), s8[4194304]{0:T(1024)(128)(4,1)S(1)}, s32[]{:S(2)}) async-start(s8[14680064]{0:T(1024)(128)(4,1)} %bitcast.35), calls=%async_computation.7 | async-start | bytes 8388608
  160.4 9.5 %slice-start.2 = ((s8[14680064]{0:T(1024)(128)(4,1)}), s8[4194304]{0:T(1024)(128)(4,1)S(1)}, s32[]{:S(2)}) async-start(s8[14680064]{0:T(1024)(128)(4,1)} %bitcast.35), calls=%async_computation.8 | async-start | bytes 8388608
  160.5 9.5 %slice-start.3 = ((s8[14680064]{0:T(1024)(128)(4,1)}), s8[2097152]{0:T(1024)(128)(4,1)S(1)}, s32[]{:S(2)}) async-start(s8[14680064]{0:T(1024)(128)(4,1)} %bitcast.35), calls=%async_computation.9 | async-start | bytes 4194304
  175.2 0.7 copy-start.5
  175.2 44.4 %copy-start.1 = (bf16[128,4096]{1,0:T(8,128)(2,1)S(1)}, bf16[128,4096]{1,0:T(8,128)(2,1)}, u32[]{:S(2)}) copy-start(bf16[128,4096]{1,0:T(8,128)(2,1)} %all-reduce.2.cloned.1.call-done) | copy-start | bytes 3145732
  175.2 102.7 %reduce-scatter.5.cloned.1.call-start = ((), (), s32[]{:S(2)}) async-start(), calls=%async_computation.5 | async-start | bytes 1114112 | tf_op jit(solution)/shard_map/reduce_scatter | solution.py:93
Sparse Core Ops, SparseCore 0:
  20.2 94.7 all-reduce.1
  119.5 32.3 all-gather.1
  175.3 41.2 reduce-scatter.2
  220.5 57.3 reduce-scatter.4
where the time goes:
time: 286 us
  waiting for transfers between devices  224 us (78%)
  matrix products  30.4 us (11%)
  between operations  13.3 us (5%)
  blocking collectives  10.7 us (4%)
  other arithmetic  6.21 us (2%)
    psum x1, waiting for transfers between devices, local(): lax.psum(placed.astype(jnp.bfloat16), ('exp', 'tp')).astype(jnp.float32)  94.5 us
    reduce_scatter x1, waiting for transfers between devices, local(): lax.psum_scatter(jnp.dot(expanded_heads, expert_wide, precision=lax.Preci...  56.8 us
    reduce_scatter x1, waiting for transfers between devices, local(): lax.psum_scatter(jnp.dot(hidden, down_matrix, preferred_element_type=jnp....  40.7 us
    all_gather x1, waiting for transfers between devices, local(): expert_input = lax.all_gather(picked, 'ctx', axis=0, tiled=True)  32.5 us
    dot_general x1, matrix products, local(): jnp.dot(expert_input, up_matrix, preferred_element_type=jnp.float32)  9.41 us
    dot_general x1, matrix products, local(): jnp.dot(expert_input, gate_matrix, preferred_element_type=jnp.float32)  8.54 us
    all_gather x1, blocking collectives, local(): key_piece = lax.all_gather(rotated_key_rows, 'ctx', axis=0, tiled=True)  5.92 us
  transfers between devices with their start and end apart: 4, of which 4 were waited for; matrix products, arithmetic and copies ran while one was open for 1% of the time, Pallas kernels for 0%

commit v1 on v0

--- a/solution.py
+++ b/solution.py
@@ -57,7 +57,7 @@
         jnp.float32
     )
     placed = lax.dynamic_update_slice_in_dim(partial_value, own_part, row_first, 0)
-    summed = lax.psum(placed.astype(jnp.bfloat16), ("exp", "tp")).astype(jnp.float32)
+    summed = lax.psum(lax.psum(placed.astype(jnp.bfloat16), "exp"), "tp").astype(jnp.float32)
     normed_block = normalize(summed, norm_gain)
     own_sum = lax.dynamic_slice_in_dim(summed, row_first, own_rows, 0)
     my_expert = lax.axis_index("exp")

time: 286 us -> 284 us (level)
    psum x1 -> x2, waiting for transfers between devices: 94.5 us -> 91.1 us  [the longest x1 53.6 us: local(): lax.psum(placed.astype(jnp.bfloat16), 'exp')]
  transfers between devices with their start and end apart: 4 -> 5, of which waited for: 4 -> 5; matrix products, arithmetic and copies ran while one was open for 1% -> 1% of each run, Pallas kernels for 0% -> 0%
where the time goes in v1:
time: 284 us
  waiting for transfers between devices  222 us (78%)
  matrix products  30.4 us (11%)
  between operations  13.3 us (5%)
  blocking collectives  10.7 us (4%)
  other arithmetic  6.25 us (2%)
    reduce_scatter x1, waiting for transfers between devices, local(): lax.psum_scatter(jnp.dot(expanded_heads, expert_wide, precision=lax.Preci...  56.8 us
    psum x1, waiting for transfers between devices, local(): lax.psum(placed.astype(jnp.bfloat16), 'exp')  53.6 us
    reduce_scatter x1, waiting for transfers between devices, local(): lax.psum_scatter(jnp.dot(hidden, down_matrix, preferred_element_type=jnp....  40.7 us
    psum x1, waiting for transfers between devices, local(): lax.psum(lax.psum(placed.astype(jnp.bfloat16), 'exp'), 'tp')  37.5 us
    all_gather x1, waiting for transfers between devices, local(): expert_input = lax.all_gather(picked, 'ctx', axis=0, tiled=True)  33.6 us
    dot_general x1, matrix products, local(): jnp.dot(expert_input, up_matrix, preferred_element_type=jnp.float32)  9.4 us
    dot_general x1, matrix products, local(): jnp.dot(expert_input, gate_matrix, preferred_element_type=jnp.float32)  8.54 us
    all_gather x1, blocking collectives, local(): key_piece = lax.all_gather(rotated_key_rows, 'ctx', axis=0, tiled=True)  5.92 us
  transfers between devices with their start and end apart: 5, of which 5 were waited for; matrix products, arithmetic and copies ran while one was open for 1% of the time, Pallas kernels for 0%

profile of v1, /device:TPU:0, one launch (start us, length us, event | category | flops | bytes accessed | tf_op | source)
XLA Modules:
  0.0 283.9 jit_solution(3553530767067413394)
XLA Ops:
  6.5 5.9 %all_gather.9 = bf16[256,128]{1,0:T(8,128)(2,1)S(1)} all-gather(bf16[128,128]{1,0:T(8,128)(2,1)} %param.12), channel_id=1, replica_groups=mesh['ctx'=2,'exp'=4,'tp'=4] {'ctx'}, dimensions={0}, use_global_device_ids=true | all-gather | bytes 98304 | tf_op jit(solution)/shard_map/all_gather | solution.py:35
  12.5 1.0 fusion.50
  13.4 4.8 %all_gather.10 = bf16[256,128]{1,0:T(8,128)(2,1)S(1)} all-gather(bf16[128,128]{1,0:T(8,128)(2,1)} %param.13), channel_id=1, replica_groups=mesh['ctx'=2,'exp'=4,'tp'=4] {'ctx'}, dimensions={0}, use_global_device_ids=true | all-gather | bytes 98304 | tf_op jit(solution)/shard_map/all_gather | solution.py:36
  18.2 0.1 fusion.22
  18.3 0.6 fusion.18
  18.9 1.2 convert_element_type.55
  20.1 0.0 all-reduce.3.cloned.1.call-update
  20.1 0.0 all-reduce.5.cloned.1.call-start
  20.2 53.6 %all-reduce.3.cloned.1.call-done = bf16[128,4096]{1,0:T(8,128)(2,1)} async-done(((bf16[128,4096]{1,0:T(8,128)(2,1)}), bf16[128,4096]{1,0:T(8,128)(2,1)}) %all-reduce.3.cloned.1.call-update) | async-done | bytes 1048592 | tf_op jit(solution)/shard_map/psum | solution.py:60
  73.8 0.0 all-reduce.5.cloned.1.call-update
  73.8 0.0 all-gather.2.cloned.1.call-start
  73.9 0.1 copy.13
  74.0 0.2 reduce-window.7
  74.2 0.1 add_reduce_fusion
  74.3 37.5 %all-reduce.5.cloned.1.call-done = bf16[128,4096]{1,0:T(8,128)(2,1)} async-done(((bf16[128,4096]{1,0:T(8,128)(2,1)}), bf16[128,4096]{1,0:T(8,128)(2,1)}) %all-reduce.5.cloned.1.call-update) | async-done | bytes 1048592 | tf_op jit(solution)/shard_map/psum | solution.py:60
  111.8 1.5 multiply_reduce_fusion
  113.3 2.7 convolution_convert_fusion.1
  116.0 0.0 all-gather.2.cloned.1.call-update
  116.1 0.0 reduce-scatter.3.cloned.1.call-start
  116.1 33.6 %all-gather.2.cloned.1.call-done = bf16[256,4096]{1,0:T(8,128)(2,1)} async-done(((bf16[128,4096]{1,0:T(8,128)(2,1)}), bf16[256,4096]{1,0:T(8,128)(2,1)}) %all-gather.2.cloned.1.call-update) | async-done | bytes 2097168 | tf_op jit(solution)/shard_map/all_gather | solution.py:74
  149.7 8.5 %fusion.4 = f32[256,1792]{1,0:T(8,128)S(1)} fusion(bf16[256,4096]{1,0:T(8,128)(2,1)} %all-gather.2.cloned.1.call-done, bf16[1,4096,1792]{2,1,0:T(8,128)(2,1)} %param.19), kind=kOutput, calls=%fused_computation.4 | convolution fusion | flops 3758096384 | bytes 18612224 | tf_op jit(solution)/shard_map/dot_general | solution.py:79
  158.3 9.4 %fusion.12 = bf16[256,1792]{1,0:T(8,128)(2,1)S(1)} fusion(bf16[256,4096]{1,0:T(8,128)(2,1)S(1)} %copy-done.6, bf16[1,4096,1792]{2,1,0:T(8,128)(2,1)} %param.20, f32[256,1792]{1,0:T(8,128)S(1)} %fusion.4), kind=kOutput, calls=%fused_computation.10 | convolution fusion | flops 3760848896 | bytes 19529728 | tf_op jit(solution)/shard_map/dot_general | solution.py:80
  167.8 5.3 %fusion.6 = bf16[256,4096]{1,0:T(8,128)(2,1)} fusion(bf16[256,1792]{1,0:T(8,128)(2,1)S(1)} %fusion.12, bf16[1,1792,4096]{2,1,0:T(8,128)(2,1)S(1)} %bitcast.36), kind=kOutput, calls=%fused_computation.6 | convolution fusion | flops 3759144960 | bytes 17694720 | tf_op jit(solution)/shard_map/dot_general | solution.py:83
  173.0 0.0 reduce-scatter.3.cloned.1.call-update
  173.1 0.0 reduce-scatter.5.cloned.1.call-start
  173.1 0.6 copy-done.5
  173.7 40.7 %reduce-scatter.3.cloned.1.call-done = bf16[32,4096]{1,0:T(8,128)(2,1)} async-done(((bf16[256,4096]{1,0:T(8,128)(2,1)}), bf16[32,4096]{1,0:T(8,128)(2,1)}) %reduce-scatter.3.cloned.1.call-update) | async-done | bytes 262160 | tf_op jit(solution)/shard_map/reduce_scatter | solution.py:82
  214.4 3.0 %convolution_convert_fusion = bf16[128,4096]{1,0:T(8,128)(2,1)} fusion(bf16[32,4096]{1,0:T(8,128)(2,1)} %reduce-scatter.3.cloned.1.call-done, f32[128]{0:T(128)S(1)} %select_reduce_fusion, s32[32]{0:T(128)S(1)} %iota_add_fusion, s32[128]{0:T(128)S(1)} %add_reduce_fusion, pred[128]{0:T(512)(128)(4,1)S(1)} %fusion.49), kind=kOutput, calls=%fused_computation.7 | convolution fusion | flops 201863168 | bytes 1312000 | tf_op jit(solution)/shard_map/dot_general | solution.py:94
  217.4 0.0 reduce-scatter.5.cloned.1.call-update
  217.4 1.6 convert_element_type.56
  219.0 56.8 %reduce-scatter.5.cloned.1.call-done = bf16[8,4096]{1,0:T(8,128)(2,1)} async-done(((bf16[128,4096]{1,0:T(8,128)(2,1)}), bf16[8,4096]{1,0:T(8,128)(2,1)}) %reduce-scatter.5.cloned.1.call-update) | async-done | bytes 65552 | tf_op jit(solution)/shard_map/reduce_scatter | solution.py:93
  275.8 1.6 add_convert_fusion
  (31 shorter events, 0.1 us)
Async XLA Ops:
  6.5 11.8 %copy-start = (bf16[128,4096]{1,0:T(8,128)(2,1)S(1)}, bf16[128,4096]{1,0:T(8,128)(2,1)}, u32[]{:S(2)}) copy-start(bf16[128,4096]{1,0:T(8,128)(2,1)} %param.16) | copy-start | bytes 3145732
  6.5 12.4 %copy-start.2 = (bf16[8,4096]{1,0:T(8,128)(2,1)S(1)}, bf16[8,4096]{1,0:T(8,128)(2,1)}, u32[]{:S(2)}) copy-start(bf16[8,4096]{1,0:T(8,128)(2,1)} %param.14) | copy-start | bytes 196612
  6.5 67.3 %all-reduce.3.cloned.1.call-start = ((), (), s32[]{:S(2)}) async-start(), calls=%async_computation.2 | async-start | bytes 2097152 | tf_op jit(solution)/shard_map/psum | solution.py:60
  18.9 54.9 %copy-start.4 = (s32[128,2]{0,1:T(2,128)S(1)}, s32[128,2]{0,1:T(2,128)}, u32[]{:S(2)}) copy-start(s32[128,2]{0,1:T(2,128)} %param.17) | copy-start | bytes 3076
  20.1 93.2 %copy-start.3 = (f32[4096]{0:T(1024)S(1)}, f32[4096]{0:T(1024)}, u32[]{:S(2)}) copy-start(f32[4096]{0:T(1024)} %param.15) | copy-start | bytes 49156
  20.1 91.6 %all-reduce.5.cloned.1.call-start = ((), (), s32[]{:S(2)}) async-start(), calls=%async_computation.3 | async-start | bytes 2097152 | tf_op jit(solution)/shard_map/psum | solution.py:60
  73.8 75.9 %all-gather.2.cloned.1.call-start = ((), (), s32[]{:S(2)}) async-start(), calls=%async_computation.4 | async-start | bytes 3145728 | tf_op jit(solution)/shard_map/all_gather | solution.py:74
  116.1 98.4 %reduce-scatter.3.cloned.1.call-start = ((), (), s32[]{:S(2)}) async-start(), calls=%async_computation.5 | async-start | bytes 2359296 | tf_op jit(solution)/shard_map/reduce_scatter | solution.py:82
  149.7 8.6 %copy-start.6 = (bf16[256,4096]{1,0:T(8,128)(2,1)S(1)}, bf16[256,4096]{1,0:T(8,128)(2,1)}, u32[]{:S(2)}) copy-start(bf16[256,4096]{1,0:T(8,128)(2,1)} %all-gather.2.cloned.1.call-done) | copy-start | bytes 6291460
  149.7 18.0 %slice-start = ((s8[14680064]{0:T(1024)(128)(4,1)}), s8[4194304]{0:T(1024)(128)(4,1)S(1)}, s32[]{:S(2)}) async-start(s8[14680064]{0:T(1024)(128)(4,1)} %bitcast.35), calls=%async_computation.7 | async-start | bytes 8388608
  149.7 18.0 %slice-start.1 = ((s8[14680064]{0:T(1024)(128)(4,1)}), s8[4194304]{0:T(1024)(128)(4,1)S(1)}, s32[]{:S(2)}) async-start(s8[14680064]{0:T(1024)(128)(4,1)} %bitcast.35), calls=%async_computation.8 | async-start | bytes 8388608
  158.3 9.5 %slice-start.2 = ((s8[14680064]{0:T(1024)(128)(4,1)}), s8[4194304]{0:T(1024)(128)(4,1)S(1)}, s32[]{:S(2)}) async-start(s8[14680064]{0:T(1024)(128)(4,1)} %bitcast.35), calls=%async_computation.9 | async-start | bytes 8388608
  158.3 9.5 %slice-start.3 = ((s8[14680064]{0:T(1024)(128)(4,1)}), s8[2097152]{0:T(1024)(128)(4,1)S(1)}, s32[]{:S(2)}) async-start(s8[14680064]{0:T(1024)(128)(4,1)} %bitcast.35), calls=%async_computation.10 | async-start | bytes 4194304
  173.0 0.7 copy-start.5
  173.0 44.4 %copy-start.1 = (bf16[128,4096]{1,0:T(8,128)(2,1)S(1)}, bf16[128,4096]{1,0:T(8,128)(2,1)}, u32[]{:S(2)}) copy-start(bf16[128,4096]{1,0:T(8,128)(2,1)} %all-reduce.5.cloned.1.call-done) | copy-start | bytes 3145732
  173.1 102.7 %reduce-scatter.5.cloned.1.call-start = ((), (), s32[]{:S(2)}) async-start(), calls=%async_computation.6 | async-start | bytes 1114112 | tf_op jit(solution)/shard_map/reduce_scatter | solution.py:93
Sparse Core Ops, SparseCore 0:
  20.3 53.4 all-reduce.2
  76.3 35.4 all-reduce.4
  116.2 33.4 all-gather.1
  173.2 41.2 reduce-scatter.2
  218.3 57.4 reduce-scatter.4
